TPU v7x, 512 devices: a whole 4x4x16 slice. The times are simulated.
512 devices in a mesh: gx: 32 (over z, x_hi), gy: 16 (over x_lo, y, core).
Axes of the slice: x: 4 (x_hi: 2, x_lo: 2; x = x_hi * 2 + x_lo), y: 4, z: 16, core: 2. Of those that a mesh axis runs over, the one named last changes fastest.
Arguments:
- source: bfloat16 [32, 16, 1280, 256], P('gx', 'gy'), may hold values from -6 to 6
- op_blocks: bfloat16 [32, 16, 10240, 128], P('gx', 'gy'), may hold values from -0.125 to 0.125
- op_in: int32 [32, 16, 80], P('gx', 'gy'), may hold values from 0 to 17, as said below
- op_out: int32 [32, 16, 80], P('gx', 'gy'), may hold values from 0 to 9, as said below
- op_count: int32 [32, 16], P('gx', 'gy'), may hold values from 24 to 80, as said below
- edge_up: int32 [32, 16, 2], P('gx', 'gy'), may hold values from 0 to 9, as said below
- edge_down: int32 [32, 16, 2], P('gx', 'gy'), may hold values from 0 to 9, as said below
Outputs:
- traces: bfloat16 [32, 16, 1280, 256], P('gx', 'gy')
Inputs may be any that keep to these rules, and one draw needn't show every extreme that they name: `op_in`: the first 18 slots of each subdomain name every input block once. `op_out`: the first 10 slots of each subdomain name every output block once. `op_count`: a multiple of 8; in every draw some subdomain has all 80 slots live. `edge_up`: distinct within a subdomain. `edge_down`: distinct within a subdomain.
All inputs are finite; a program needn't handle non-finite values.
Results may differ from a plain program's by a relative error of at most 0.0039.
Values may be sent and summed in bfloat16 or wider, within the bound.
A program may use at most 128 MiB of HBM per device.

v0:
```python
import jax
import jax.numpy as jnp
from jax import lax
from jax.sharding import PartitionSpec as P

FX = 2
EMAX = 2
ITERS = 4


def from_behind(block, axis, distance):
    devices = range(lax.axis_size(axis))
    route = [((i - distance) % len(devices), i) for i in devices]
    return lax.ppermute(block, axis, route)


def shifted(value, axis, steps):
    count = lax.axis_size(axis)
    initial, last = (max(0, -steps), min(count, count - steps))
    return lax.ppermute(value, axis, [(source, source + steps) for source in range(initial, last)])


def gather_inputs(trace_rows, up_index, down_index, block_size):
    row_count = trace_rows.shape[0]
    columns = trace_rows.shape[1]
    block_count = row_count // block_size
    face_rows = FX * block_size
    from_left = from_behind(trace_rows[row_count - face_rows :], "gx", 1)
    from_right = from_behind(trace_rows[:face_rows], "gx", -1)
    framed = jnp.concatenate([from_left, trace_rows, from_right], axis=0)
    trace_blocks = trace_rows.reshape(block_count, block_size, columns)
    edge_rows = EMAX * block_size
    up_pick = trace_blocks[up_index].reshape(edge_rows, columns)
    down_pick = trace_blocks[down_index].reshape(edge_rows, columns)
    from_below = shifted(up_pick, "gy", 1)
    from_above = shifted(down_pick, "gy", -1)
    inputs = jnp.concatenate([framed, from_below, from_above], axis=0)
    return inputs.reshape(-1, block_size, columns)


def slots_term(totals, block_now, in_now, out_now, live_mask, inputs):
    block_count = totals.shape[0]
    picked = inputs[in_now]
    products = jnp.einsum("ekm,emr->ekr", block_now, picked, preferred_element_type=jnp.float32)
    block_ids = jnp.arange(block_count, dtype=jnp.int32)
    onehot = ((out_now[:, None] == block_ids[None, :]) & live_mask[:, None]).astype(jnp.float32)
    return jnp.einsum("eb,ekr->bkr", onehot, products, precision=lax.Precision.HIGHEST)


def shards(source, op_blocks, op_in, op_out, op_count, edge_up, edge_down):
    row_count = source.shape[2]
    columns = source.shape[3]
    block_size = op_blocks.shape[3]
    block_count = row_count // block_size
    slot_total = op_in.shape[2]
    source_rows = source.reshape(row_count, columns)
    all_blocks = op_blocks.reshape(slot_total, block_size, block_size)
    all_in = op_in.reshape(slot_total)
    all_out = op_out.reshape(slot_total)
    live_count = op_count.reshape(())
    up_index = edge_up.reshape(-1)
    down_index = edge_down.reshape(-1)
    slot_numbers = jnp.arange(slot_total, dtype=jnp.int32)
    source_blocks = source_rows.reshape(block_count, block_size, columns).astype(jnp.float32)
    trace_rows = source_rows
    for sweep_index in range(ITERS):
        inputs = gather_inputs(trace_rows, up_index, down_index, block_size)
        empty = jnp.zeros((block_count, block_size, columns), jnp.float32)
        live_mask = slot_numbers < live_count
        totals = slots_term(empty, all_blocks, all_in, all_out, live_mask, inputs)
        trace_rows = (source_blocks + totals).astype(jnp.bfloat16).reshape(row_count, columns)
    return trace_rows.reshape(source.shape)


def solution(mesh):
    placed = (
        P("gx", "gy", None, None),
        P("gx", "gy", None, None),
        P("gx", "gy", None),
        P("gx", "gy", None),
        P("gx", "gy"),
        P("gx", "gy", None),
        P("gx", "gy", None),
    )
    return jax.shard_map(
        shards, mesh=mesh, in_specs=placed, out_specs=P("gx", "gy", None, None), check_vma=False
    )
```

profile of v0, /device:TPU:25, one launch (start us, length us, event | category | flops | bytes accessed | tf_op | source)
XLA Modules:
  0.0 264.3 jit_solution(12893721845449154134)
XLA Ops:
  3.1 3.3 %collective-permute-start.2 = (bf16[256,256]{1,0:T(8,128)(2,1)S(1)}, bf16[256,256]{1,0:T(8,128)(2,1)S(1)}, u32[]{:S(2)}, u32[]{:S(2)}) collective-permute-start(bf16[256,256]{1,0:T(8,128)(2,1)S(1)} %bitcast.93), channel_id=1, source_target_pairs={{0,1},{1,2},{2,3},{3,4},{4,5},{5,6},{6,7},{7,8},{8,9},{9,10},{10,1... | collective-permute-start | bytes 393224 | tf_op jit(solution)/shard_map/ppermute | solution.py:20
  11.0 13.3 %collective-permute-start.1 = (bf16[256,256]{1,0:T(8,128)(2,1)S(1)}, bf16[256,256]{1,0:T(8,128)(2,1)S(1)}, u32[]{:S(2)}, u32[]{:S(2)}) collective-permute-start(bf16[256,256]{1,0:T(8,128)(2,1)S(1)} %get-tuple-element.11), channel_id=1, source_target_pairs={{16,0},{32,16},{48,32},{64,48},{80,64},{96,80},{112,96},{128,112},... | collective-permute-start | bytes 393224 | tf_op jit(solution)/shard_map/ppermute | solution.py:14
  27.6 6.1 %collective-permute-done = bf16[256,256]{1,0:T(8,128)(2,1)S(1)} collective-permute-done((bf16[256,256]{1,0:T(8,128)(2,1)S(1)}, bf16[256,256]{1,0:T(8,128)(2,1)S(1)}, u32[]{:S(2)}, u32[]{:S(2)}) %collective-permute-start) | collective-permute-done | bytes 131104 | tf_op jit(solution)/shard_map/ppermute | solution.py:14
  34.3 2.0 bitcast_dynamic-update-slice_fusion
  38.3 7.0 %gather_fusion.2 = bf16[80,128,256]{2,1,0:T(8,128)(2,1)} fusion(bf16[18,128,256]{2,1,0:T(8,128)(2,1)} %bitcast.13, s32[1024]{0:T(1024)S(1)} %pad_clamp_fusion), kind=kCustom, calls=%fused_computation.2 | custom fusion | bytes 10486080 | tf_op jit(solution)/shard_map/gather | solution.py:43
  45.2 8.1 %fusion.32 = f32[80,256,128]{2,1,0:T(8,128)} fusion(bf16[80,128,256]{2,1,0:T(8,128)(2,1)} %gather_fusion.2, bf16[80,128,128]{2,1,0:T(8,128)(2,1)S(1)} %bitcast.79), kind=kOutput, calls=%fused_computation.66 | convolution fusion | flops 671088640 | bytes 18350080 | tf_op jit(solution)/shard_map/ekm,emr->ekr/dot_general | solution.py:44
  53.3 11.7 %copy.25 = f32[80,256,128]{1,0,2:T(8,128)} copy(f32[80,256,128]{2,1,0:T(8,128)} %fusion.32) | data formatting | bytes 20971520 | tf_op jit(solution)/shard_map/ekm,emr->ekr/dot_general | solution.py:44
  65.0 7.8 %fusion.8 = bf16[10,128,256]{2,0,1:T(8,128)(2,1)S(1)} fusion(f32[80,256,128]{1,0,2:T(8,128)} %copy.25, bf16[10,128,256]{2,1,0:T(8,128)(2,1)S(1)} %bitcast.85, s32[80]{0:T(128)S(1)} %bitcast.103, pred[80]{0:T(512)(128)(4,1)S(1)} %iota_compare_fusion.1), kind=kOutput, calls=%fused_computation.24 | convolution fusion | flops 315557440 | bytes 11796880 | tf_op jit(solution)/shard_map/eb,ekr->bkr/dot_general | solution.py:47
  78.2 2.3 gather_fusion.3
  80.5 6.6 %collective-permute-start.6 = (bf16[256,256]{1,0:T(8,128)(2,1)}, bf16[256,256]{1,0:T(8,128)(2,1)S(1)}, u32[]{:S(2)}, u32[]{:S(2)}) collective-permute-start(bf16[256,256]{1,0:T(8,128)(2,1)} %bitcast.98), channel_id=1, source_target_pairs={{0,1},{1,2},{2,3},{3,4},{4,5},{5,6},{6,7},{7,8},{8,9},{9,10},{10,1... | collective-permute-start | bytes 393224 | tf_op jit(solution)/shard_map/ppermute | solution.py:20
  89.0 8.0 %collective-permute-start.5 = (bf16[256,256]{1,0:T(8,128)(2,1)S(1)}, bf16[256,256]{1,0:T(8,128)(2,1)S(1)}, u32[]{:S(2)}, u32[]{:S(2)}) collective-permute-start(bf16[256,256]{1,0:T(8,128)(2,1)S(1)} %bitcast.100), channel_id=1, source_target_pairs={{16,0},{32,16},{48,32},{64,48},{80,64},{96,80},{112,96},{128,112},... | collective-permute-start | bytes 393224 | tf_op jit(solution)/shard_map/ppermute | solution.py:14
  98.6 2.0 constant_dynamic-update-slice_fusion.7
  102.6 7.0 %gather_fusion.5 = bf16[80,128,256]{2,1,0:T(8,128)(2,1)} fusion(bf16[18,128,256]{2,1,0:T(8,128)(2,1)} %bitcast.23, s32[1024]{0:T(1024)S(1)} %pad_clamp_fusion), kind=kCustom, calls=%fused_computation.5 | custom fusion | bytes 10486080 | tf_op jit(solution)/shard_map/gather | solution.py:43
  109.5 8.1 %fusion.33 = f32[80,256,128]{2,1,0:T(8,128)} fusion(bf16[80,128,256]{2,1,0:T(8,128)(2,1)} %gather_fusion.5, bf16[80,128,128]{2,1,0:T(8,128)(2,1)S(1)} %bitcast.80), kind=kOutput, calls=%fused_computation.67 | convolution fusion | flops 671088640 | bytes 18350080 | tf_op jit(solution)/shard_map/ekm,emr->ekr/dot_general | solution.py:44
  117.6 11.6 %copy.26 = f32[80,256,128]{1,0,2:T(8,128)} copy(f32[80,256,128]{2,1,0:T(8,128)} %fusion.33) | data formatting | bytes 20971520 | tf_op jit(solution)/shard_map/ekm,emr->ekr/dot_general | solution.py:44
  129.2 7.8 %fusion.9 = bf16[10,128,256]{2,0,1:T(8,128)(2,1)S(1)} fusion(f32[80,256,128]{1,0,2:T(8,128)} %copy.26, bf16[10,128,256]{2,1,0:T(8,128)(2,1)S(1)} %bitcast.86, s32[80]{0:T(128)S(1)} %bitcast.104, pred[80]{0:T(512)(128)(4,1)S(1)} %copy-done.4), kind=kOutput, calls=%fused_computation.25 | convolution fusion | flops 315557440 | bytes 11796880 | tf_op jit(solution)/shard_map/eb,ekr->bkr/dot_general | solution.py:47
  142.4 2.3 gather_fusion.6
  144.7 5.4 %collective-permute-start.10 = (bf16[256,256]{1,0:T(8,128)(2,1)}, bf16[256,256]{1,0:T(8,128)(2,1)S(1)}, u32[]{:S(2)}, u32[]{:S(2)}) collective-permute-start(bf16[256,256]{1,0:T(8,128)(2,1)} %bitcast.99), channel_id=1, source_target_pairs={{0,1},{1,2},{2,3},{3,4},{4,5},{5,6},{6,7},{7,8},{8,9},{9,10},{10,1... | collective-permute-start | bytes 393224 | tf_op jit(solution)/shard_map/ppermute | solution.py:20
  152.1 8.1 %collective-permute-start.9 = (bf16[256,256]{1,0:T(8,128)(2,1)S(1)}, bf16[256,256]{1,0:T(8,128)(2,1)S(1)}, u32[]{:S(2)}, u32[]{:S(2)}) collective-permute-start(bf16[256,256]{1,0:T(8,128)(2,1)S(1)} %bitcast.101), channel_id=1, source_target_pairs={{16,0},{32,16},{48,32},{64,48},{80,64},{96,80},{112,96},{128,112},... | collective-permute-start | bytes 393224 | tf_op jit(solution)/shard_map/ppermute | solution.py:14
  161.7 2.0 constant_dynamic-update-slice_fusion.12
  165.7 7.0 %gather_fusion.8 = bf16[80,128,256]{2,1,0:T(8,128)(2,1)} fusion(bf16[18,128,256]{2,1,0:T(8,128)(2,1)} %bitcast.30, s32[1024]{0:T(1024)S(1)} %pad_clamp_fusion), kind=kCustom, calls=%fused_computation.8 | custom fusion | bytes 10486080 | tf_op jit(solution)/shard_map/gather | solution.py:43
  172.6 8.1 %fusion.34 = f32[80,256,128]{2,1,0:T(8,128)} fusion(bf16[80,128,256]{2,1,0:T(8,128)(2,1)} %gather_fusion.8, bf16[80,128,128]{2,1,0:T(8,128)(2,1)S(1)} %bitcast.81), kind=kOutput, calls=%fused_computation.68 | convolution fusion | flops 671088640 | bytes 18350080 | tf_op jit(solution)/shard_map/ekm,emr->ekr/dot_general | solution.py:44
  180.7 11.6 %copy.27 = f32[80,256,128]{1,0,2:T(8,128)} copy(f32[80,256,128]{2,1,0:T(8,128)} %fusion.34) | data formatting | bytes 20971520 | tf_op jit(solution)/shard_map/ekm,emr->ekr/dot_general | solution.py:44
  192.3 7.8 %fusion.10 = bf16[10,128,256]{2,0,1:T(8,128)(2,1)S(1)} fusion(f32[80,256,128]{1,0,2:T(8,128)} %copy.27, bf16[10,128,256]{2,1,0:T(8,128)(2,1)S(1)} %bitcast.87, s32[80]{0:T(128)S(1)} %bitcast.105, pred[80]{0:T(512)(128)(4,1)S(1)} %copy-done.5), kind=kOutput, calls=%fused_computation.26 | convolution fusion | flops 315557440 | bytes 11796880 | tf_op jit(solution)/shard_map/eb,ekr->bkr/dot_general | solution.py:47
  205.5 2.3 gather_fusion.9
  207.8 5.4 %collective-permute-start.14 = (bf16[256,256]{1,0:T(8,128)(2,1)}, bf16[256,256]{1,0:T(8,128)(2,1)S(1)}, u32[]{:S(2)}, u32[]{:S(2)}) collective-permute-start(bf16[256,256]{1,0:T(8,128)(2,1)} %bitcast.97), channel_id=1, source_target_pairs={{0,1},{1,2},{2,3},{3,4},{4,5},{5,6},{6,7},{7,8},{8,9},{9,10},{10,1... | collective-permute-start | bytes 393224 | tf_op jit(solution)/shard_map/ppermute | solution.py:20
  215.2 8.1 %collective-permute-start.13 = (bf16[256,256]{1,0:T(8,128)(2,1)S(1)}, bf16[256,256]{1,0:T(8,128)(2,1)S(1)}, u32[]{:S(2)}, u32[]{:S(2)}) collective-permute-start(bf16[256,256]{1,0:T(8,128)(2,1)S(1)} %bitcast.102), channel_id=1, source_target_pairs={{16,0},{32,16},{48,32},{64,48},{80,64},{96,80},{112,96},{128,112},... | collective-permute-start | bytes 393224 | tf_op jit(solution)/shard_map/ppermute | solution.py:14
  224.9 2.0 constant_dynamic-update-slice_fusion.17
  228.8 7.0 %gather_fusion.11 = bf16[80,128,256]{2,1,0:T(8,128)(2,1)} fusion(bf16[18,128,256]{2,1,0:T(8,128)(2,1)} %bitcast.37, s32[1024]{0:T(1024)S(1)} %pad_clamp_fusion), kind=kCustom, calls=%fused_computation.11 | custom fusion | bytes 10486080 | tf_op jit(solution)/shard_map/gather | solution.py:43
  235.8 8.1 %fusion.35 = f32[80,256,128]{2,1,0:T(8,128)} fusion(bf16[80,128,256]{2,1,0:T(8,128)(2,1)} %gather_fusion.11, bf16[80,128,128]{2,1,0:T(8,128)(2,1)S(1)} %bitcast.82), kind=kOutput, calls=%fused_computation.69 | convolution fusion | flops 671088640 | bytes 18350080 | tf_op jit(solution)/shard_map/ekm,emr->ekr/dot_general | solution.py:44
  243.8 11.6 %copy.28 = f32[80,256,128]{1,0,2:T(8,128)} copy(f32[80,256,128]{2,1,0:T(8,128)} %fusion.35) | data formatting | bytes 20971520 | tf_op jit(solution)/shard_map/ekm,emr->ekr/dot_general | solution.py:44
  255.4 7.8 %fusion.11 = bf16[10,128,256]{2,0,1:T(8,128)(2,1)S(1)} fusion(f32[80,256,128]{1,0,2:T(8,128)} %copy.28, bf16[10,128,256]{2,1,0:T(8,128)(2,1)S(1)} %bitcast.88, s32[80]{0:T(128)S(1)} %bitcast.106, pred[80]{0:T(512)(128)(4,1)S(1)} %copy-done.6), kind=kOutput, calls=%fused_computation.27 | convolution fusion | flops 315557440 | bytes 11796880 | tf_op jit(solution)/shard_map/eb,ekr->bkr/dot_general | solution.py:47
  (78 shorter events, 46.5 us)
Async XLA Ops:
  0.0 45.2 %copy-start = (bf16[1,1,10240,128]{3,2,1,0:T(8,128)(2,1)S(1)}, bf16[1,1,10240,128]{3,2,1,0:T(8,128)(2,1)}, u32[]{:S(2)}) copy-start(bf16[1,1,10240,128]{3,2,1,0:T(8,128)(2,1)} %param.8) | copy-start | bytes 7864324
  3.1 33.8 %collective-permute-start.2 = (bf16[256,256]{1,0:T(8,128)(2,1)S(1)}, bf16[256,256]{1,0:T(8,128)(2,1)S(1)}, u32[]{:S(2)}, u32[]{:S(2)}) collective-permute-start(bf16[256,256]{1,0:T(8,128)(2,1)S(1)} %bitcast.93), channel_id=1, source_target_pairs={{0,1},{1,2},{2,3},{3,4},{4,5},{5,6},{6,7},{7,8},{8,9},{9,10},{10,1... | collective-permute-start | bytes 393224 | tf_op jit(solution)/shard_map/ppermute | solution.py:20
  8.1 29.5 %collective-permute-start.3 = (bf16[256,256]{1,0:T(8,128)(2,1)S(1)}, bf16[256,256]{1,0:T(8,128)(2,1)S(1)}, u32[]{:S(2)}, u32[]{:S(2)}) collective-permute-start(bf16[256,256]{1,0:T(8,128)(2,1)S(1)} %bitcast.92), channel_id=1, source_target_pairs={{1,0},{2,1},{3,2},{4,3},{5,4},{6,5},{7,6},{8,7},{9,8},{10,9},{11,1... | collective-permute-start | bytes 393224 | tf_op jit(solution)/shard_map/ppermute | solution.py:20
  11.0 25.3 %collective-permute-start.1 = (bf16[256,256]{1,0:T(8,128)(2,1)S(1)}, bf16[256,256]{1,0:T(8,128)(2,1)S(1)}, u32[]{:S(2)}, u32[]{:S(2)}) collective-permute-start(bf16[256,256]{1,0:T(8,128)(2,1)S(1)} %get-tuple-element.11), channel_id=1, source_target_pairs={{16,0},{32,16},{48,32},{64,48},{80,64},{96,80},{112,96},{128,112},... | collective-permute-start | bytes 393224 | tf_op jit(solution)/shard_map/ppermute | solution.py:14
  24.3 9.3 %collective-permute-start = (bf16[256,256]{1,0:T(8,128)(2,1)S(1)}, bf16[256,256]{1,0:T(8,128)(2,1)S(1)}, u32[]{:S(2)}, u32[]{:S(2)}) collective-permute-start(bf16[256,256]{1,0:T(8,128)(2,1)S(1)} %get-tuple-element.12), channel_id=1, source_target_pairs={{496,0},{0,16},{16,32},{32,48},{48,64},{64,80},{80,96},{96,112},{1... | collective-permute-start | bytes 393224 | tf_op jit(solution)/shard_map/ppermute | solution.py:14
  27.6 37.4 %copy-start.3 = (pred[80]{0:T(512)(128)(4,1)}, pred[80]{0:T(512)(128)(4,1)S(1)}, u32[]{:S(2)}) copy-start(pred[80]{0:T(512)(128)(4,1)S(1)} %iota_compare_fusion.1) | copy-start | bytes 244
  53.3 11.7 %copy-start.1 = (bf16[1,1,1280,256]{3,2,1,0:T(8,128)(2,1)S(1)}, bf16[1,1,1280,256]{3,2,1,0:T(8,128)(2,1)}, u32[]{:S(2)}) copy-start(bf16[1,1,1280,256]{3,2,1,0:T(8,128)(2,1)} %param.7) | copy-start | bytes 1966084
  53.3 11.7 %copy-start.2 = (s32[1,1,80]{2,1,0:T(1,128)S(1)}, s32[1,1,80]{2,1,0:T(1,128)}, u32[]{:S(2)}) copy-start(s32[1,1,80]{2,1,0:T(1,128)} %param.10) | copy-start | bytes 964
  73.6 23.5 %collective-permute-start.4 = (bf16[256,256]{1,0:T(8,128)(2,1)}, bf16[256,256]{1,0:T(8,128)(2,1)}, u32[]{:S(2)}, u32[]{:S(2)}) collective-permute-start(bf16[256,256]{1,0:T(8,128)(2,1)} %bitcast.18), channel_id=1, source_target_pairs={{496,0},{0,16},{16,32},{32,48},{48,64},{64,80},{80,96},{96,112},{1... | collective-permute-start | bytes 393224 | tf_op jit(solution)/shard_map/ppermute | solution.py:14
  80.5 20.7 %collective-permute-start.6 = (bf16[256,256]{1,0:T(8,128)(2,1)}, bf16[256,256]{1,0:T(8,128)(2,1)S(1)}, u32[]{:S(2)}, u32[]{:S(2)}) collective-permute-start(bf16[256,256]{1,0:T(8,128)(2,1)} %bitcast.98), channel_id=1, source_target_pairs={{0,1},{1,2},{2,3},{3,4},{4,5},{5,6},{6,7},{7,8},{8,9},{9,10},{10,1... | collective-permute-start | bytes 393224 | tf_op jit(solution)/shard_map/ppermute | solution.py:20
  87.1 14.8 %collective-permute-start.7 = (bf16[256,256]{1,0:T(8,128)(2,1)S(1)}, bf16[256,256]{1,0:T(8,128)(2,1)S(1)}, u32[]{:S(2)}, u32[]{:S(2)}) collective-permute-start(bf16[256,256]{1,0:T(8,128)(2,1)S(1)} %bitcast.95), channel_id=1, source_target_pairs={{1,0},{2,1},{3,2},{4,3},{5,4},{6,5},{7,6},{8,7},{9,8},{10,9},{11,1... | collective-permute-start | bytes 393224 | tf_op jit(solution)/shard_map/ppermute | solution.py:20
  89.0 11.6 %collective-permute-start.5 = (bf16[256,256]{1,0:T(8,128)(2,1)S(1)}, bf16[256,256]{1,0:T(8,128)(2,1)S(1)}, u32[]{:S(2)}, u32[]{:S(2)}) collective-permute-start(bf16[256,256]{1,0:T(8,128)(2,1)S(1)} %bitcast.100), channel_id=1, source_target_pairs={{16,0},{32,16},{48,32},{64,48},{80,64},{96,80},{112,96},{128,112},... | collective-permute-start | bytes 393224 | tf_op jit(solution)/shard_map/ppermute | solution.py:14
  117.6 11.6 %copy-start.4 = (pred[80]{0:T(512)(128)(4,1)S(1)}, pred[80]{0:T(512)(128)(4,1)}, u32[]{:S(2)}) copy-start(pred[80]{0:T(512)(128)(4,1)} %copy-done.3) | copy-start | bytes 244
  137.8 22.4 %collective-permute-start.8 = (bf16[256,256]{1,0:T(8,128)(2,1)}, bf16[256,256]{1,0:T(8,128)(2,1)}, u32[]{:S(2)}, u32[]{:S(2)}) collective-permute-start(bf16[256,256]{1,0:T(8,128)(2,1)} %bitcast.25), channel_id=1, source_target_pairs={{496,0},{0,16},{16,32},{32,48},{48,64},{64,80},{80,96},{96,112},{1... | collective-permute-start | bytes 393224 | tf_op jit(solution)/shard_map/ppermute | solution.py:14
  144.7 19.6 %collective-permute-start.10 = (bf16[256,256]{1,0:T(8,128)(2,1)}, bf16[256,256]{1,0:T(8,128)(2,1)S(1)}, u32[]{:S(2)}, u32[]{:S(2)}) collective-permute-start(bf16[256,256]{1,0:T(8,128)(2,1)} %bitcast.99), channel_id=1, source_target_pairs={{0,1},{1,2},{2,3},{3,4},{4,5},{5,6},{6,7},{7,8},{8,9},{9,10},{10,1... | collective-permute-start | bytes 393224 | tf_op jit(solution)/shard_map/ppermute | solution.py:20
  150.1 14.9 %collective-permute-start.11 = (bf16[256,256]{1,0:T(8,128)(2,1)S(1)}, bf16[256,256]{1,0:T(8,128)(2,1)S(1)}, u32[]{:S(2)}, u32[]{:S(2)}) collective-permute-start(bf16[256,256]{1,0:T(8,128)(2,1)S(1)} %bitcast.96), channel_id=1, source_target_pairs={{1,0},{2,1},{3,2},{4,3},{5,4},{6,5},{7,6},{8,7},{9,8},{10,9},{11,1... | collective-permute-start | bytes 393224 | tf_op jit(solution)/shard_map/ppermute | solution.py:20
  152.1 11.6 %collective-permute-start.9 = (bf16[256,256]{1,0:T(8,128)(2,1)S(1)}, bf16[256,256]{1,0:T(8,128)(2,1)S(1)}, u32[]{:S(2)}, u32[]{:S(2)}) collective-permute-start(bf16[256,256]{1,0:T(8,128)(2,1)S(1)} %bitcast.101), channel_id=1, source_target_pairs={{16,0},{32,16},{48,32},{64,48},{80,64},{96,80},{112,96},{128,112},... | collective-permute-start | bytes 393224 | tf_op jit(solution)/shard_map/ppermute | solution.py:14
  180.7 11.6 %copy-start.5 = (pred[80]{0:T(512)(128)(4,1)S(1)}, pred[80]{0:T(512)(128)(4,1)}, u32[]{:S(2)}) copy-start(pred[80]{0:T(512)(128)(4,1)} %copy-done.3) | copy-start | bytes 244
  200.9 22.4 %collective-permute-start.12 = (bf16[256,256]{1,0:T(8,128)(2,1)}, bf16[256,256]{1,0:T(8,128)(2,1)}, u32[]{:S(2)}, u32[]{:S(2)}) collective-permute-start(bf16[256,256]{1,0:T(8,128)(2,1)} %bitcast.32), channel_id=1, source_target_pairs={{496,0},{0,16},{16,32},{32,48},{48,64},{64,80},{80,96},{96,112},{1... | collective-permute-start | bytes 393224 | tf_op jit(solution)/shard_map/ppermute | solution.py:14
  207.8 19.7 %collective-permute-start.14 = (bf16[256,256]{1,0:T(8,128)(2,1)}, bf16[256,256]{1,0:T(8,128)(2,1)S(1)}, u32[]{:S(2)}, u32[]{:S(2)}) collective-permute-start(bf16[256,256]{1,0:T(8,128)(2,1)} %bitcast.97), channel_id=1, source_target_pairs={{0,1},{1,2},{2,3},{3,4},{4,5},{5,6},{6,7},{7,8},{8,9},{9,10},{10,1... | collective-permute-start | bytes 393224 | tf_op jit(solution)/shard_map/ppermute | solution.py:20
  213.2 14.9 %collective-permute-start.15 = (bf16[256,256]{1,0:T(8,128)(2,1)S(1)}, bf16[256,256]{1,0:T(8,128)(2,1)S(1)}, u32[]{:S(2)}, u32[]{:S(2)}) collective-permute-start(bf16[256,256]{1,0:T(8,128)(2,1)S(1)} %bitcast.94), channel_id=1, source_target_pairs={{1,0},{2,1},{3,2},{4,3},{5,4},{6,5},{7,6},{8,7},{9,8},{10,9},{11,1... | collective-permute-start | bytes 393224 | tf_op jit(solution)/shard_map/ppermute | solution.py:20
  215.2 11.7 %collective-permute-start.13 = (bf16[256,256]{1,0:T(8,128)(2,1)S(1)}, bf16[256,256]{1,0:T(8,128)(2,1)S(1)}, u32[]{:S(2)}, u32[]{:S(2)}) collective-permute-start(bf16[256,256]{1,0:T(8,128)(2,1)S(1)} %bitcast.102), channel_id=1, source_target_pairs={{16,0},{32,16},{48,32},{64,48},{80,64},{96,80},{112,96},{128,112},... | collective-permute-start | bytes 393224 | tf_op jit(solution)/shard_map/ppermute | solution.py:14
  243.8 11.6 %copy-start.6 = (pred[80]{0:T(512)(128)(4,1)S(1)}, pred[80]{0:T(512)(128)(4,1)}, u32[]{:S(2)}) copy-start(pred[80]{0:T(512)(128)(4,1)} %copy-done.3) | copy-start | bytes 244
where the time goes:
time: 269 us; the launch traced here: 264 us
  local copies, waits for them, and re-layouts  118 us (44%)
  starting transfers between devices  73.6 us (27%)
  matrix products  63.5 us (24%)
  waiting for transfers between devices  6.11 us (2%)
    dot_general x4, local copies, waits for them, and re-layouts, slots_term(): jnp.einsum('ekm,emr->ekr', block_now, picked, preferred_element_type=jnp....  46.5 us
    ppermute x8, starting transfers between devices, from_behind(): return lax.ppermute(block, axis, route)  45.2 us
    dot_general x4, matrix products, slots_term(): jnp.einsum('ekm,emr->ekr', block_now, picked, preferred_element_type=jnp....  32.3 us
    dot_general x4, matrix products, slots_term(): jnp.einsum('eb,ekr->bkr', onehot, products, precision=lax.Precision.HIGHEST)  31.2 us
    ppermute x8, starting transfers between devices, shifted(): lax.ppermute(value, axis, [(source, source + steps) for source in range(i...  28.4 us
    gather x4, local copies, waits for them, and re-layouts, slots_term(): picked = inputs[in_now]  27.8 us
    unnamed x30, local copies, waits for them, and re-layouts  18.5 us
    gather x4, local copies, waits for them, and re-layouts, gather_inputs(): up_pick = trace_blocks[up_index].reshape(edge_rows, columns)  8.51 us
  transfers between devices with their start and end apart: 16, of which 1 were waited for; matrix products, arithmetic and copies ran while one was open for 14% of the time, Pallas kernels for 0%

commit v1 on v0

v1 whole, which is shorter than its diff:
```python
import functools

import jax
import jax.numpy as jnp
from jax import lax
from jax.experimental import pallas as pl
from jax.experimental.pallas import tpu as pltpu
from jax.sharding import PartitionSpec as P

FX = 2
EMAX = 2
ITERS = 4
CHUNKS = 2
MESH = pl.DeviceIdType.MESH


def merge_kernel(ops_in, ops_out, count, blocks, dense, sums, merged, last):
    slots, bs = blocks.shape[0], blocks.shape[1]
    nb, ni = dense.shape[0] // bs, dense.shape[1] // bs
    live = count[0, 0]

    def clear(cell, carry):
        last[cell] = slots
        return carry

    lax.fori_loop(0, nb * ni + 1, clear, 0, unroll=8)
    sums[slots] = jnp.zeros((bs, bs), jnp.float32)
    merged[slots] = jnp.zeros((bs, bs), merged.dtype)

    def add(s, carry):
        cell = jnp.where(s < live, ops_out[0, s] * ni + ops_in[0, s], nb * ni)
        total = sums[last[cell]] + blocks[s].astype(jnp.float32)
        last[cell] = s
        sums[s] = total
        merged[s] = total.astype(merged.dtype)
        return carry

    lax.fori_loop(0, slots, add, 0, unroll=4)

    def fill(j, carry):
        for i in range(ni):
            at = i - FX if FX <= i < FX + nb else (nb + i if i < FX else i)
            dense[pl.ds(j * bs, bs), at * bs : (at + 1) * bs] = merged[last[j * ni + i]]
        return carry

    lax.fori_loop(0, nb, fill, 0)


def sweep_kernel(
    sizes, source, dense, ups, downs, result,
    trace, faces_in, edges_in, up_pick, down_pick, own_sum, final,
    load_sem, store_sem, send_sem, recv_sem,
):
    n_gx, n_gy = sizes
    nb, bs, width = trace.shape[2:]
    rows, face, edge = nb * bs, FX * bs, EMAX * bs
    gx, gy = lax.axis_index("gx"), lax.axis_index("gy")
    right = (lax.rem(gx + 1, n_gx), gy)
    left = (lax.rem(gx + n_gx - 1, n_gx), gy)
    above = (gx, lax.rem(gy + 1, n_gy))
    below = (gx, lax.rem(gy + n_gy - 1, n_gy))
    has_above, has_below = gy < n_gy - 1, gy > 0

    barrier = pltpu.get_barrier_semaphore()
    for place in (right, left):
        pl.semaphore_signal(barrier, inc=1, device_id=place, device_id_type=MESH)

    @pl.when(has_above)
    def _():
        pl.semaphore_signal(barrier, inc=1, device_id=above, device_id_type=MESH)

    @pl.when(has_below)
    def _():
        pl.semaphore_signal(barrier, inc=1, device_id=below, device_id_type=MESH)

    loads = [
        pltpu.make_async_copy(
            source.at[:, :, pl.ds(c * width, width)], trace.at[0, c], load_sem.at[c]
        )
        for c in range(CHUNKS)
    ]
    for copy in loads:
        copy.start()

    @pl.when(jnp.logical_not(has_below))
    def _():
        edges_in[:, :, 0:EMAX] = jnp.zeros((ITERS, CHUNKS, EMAX, bs, width), edges_in.dtype)

    @pl.when(jnp.logical_not(has_above))
    def _():
        edges_in[:, :, EMAX:] = jnp.zeros((ITERS, CHUNKS, EMAX, bs, width), edges_in.dtype)

    def remote(t, c, which):
        src, dst, place = (
            (trace.at[t, c, pl.ds(nb - FX, FX)], faces_in.at[t, c, pl.ds(0, FX)], right),
            (trace.at[t, c, pl.ds(0, FX)], faces_in.at[t, c, pl.ds(FX, FX)], left),
            (up_pick.at[t, c], edges_in.at[t, c, pl.ds(0, EMAX)], above),
            (down_pick.at[t, c], edges_in.at[t, c, pl.ds(EMAX, EMAX)], below),
        )[which]
        return pltpu.make_async_remote_copy(
            src_ref=src,
            dst_ref=dst,
            send_sem=send_sem.at[t, c, which],
            recv_sem=recv_sem.at[t, c, which],
            device_id=place,
            device_id_type=MESH,
        )

    def send_edges(t, c):
        @pl.when(has_above)
        def _():
            for k in range(EMAX):
                up_pick[t, c, k] = trace[t, c, ups[0, k]]
            remote(t, c, 2).start()

        @pl.when(has_below)
        def _():
            for k in range(EMAX):
                down_pick[t, c, k] = trace[t, c, downs[0, k]]
            remote(t, c, 3).start()

    def dot(first_row, end_row, first, size, inputs):
        return jnp.dot(
            dense[first_row:end_row, first : first + size],
            inputs.reshape(size, width),
            preferred_element_type=jnp.float32,
        )

    def own_term(t, c):
        terms = trace[0, c].reshape(rows, width).astype(jnp.float32)
        own_sum[c] = terms + dot(0, rows, 0, rows, trace[t, c])

    for copy in loads:
        copy.wait()
    pl.semaphore_wait(barrier, 2 + has_above.astype(jnp.int32) + has_below.astype(jnp.int32))
    for c in range(CHUNKS):
        remote(0, c, 0).start()
        remote(0, c, 1).start()
        send_edges(0, c)
    for c in range(CHUNKS):
        own_term(0, c)

    for t in range(ITERS):
        for c in range(CHUNKS):
            @pl.when(has_below)
            def _():
                remote(t, c, 2).wait_recv()

            @pl.when(has_above)
            def _():
                remote(t, c, 3).wait_recv()

            own_sum[c] += dot(0, rows, rows + 2 * face, 2 * edge, edges_in[t, c])
            remote(t, c, 0).wait_recv()
            remote(t, c, 1).wait_recv()

            def finish(first_row, end_row):
                total = own_sum[c, first_row:end_row] + dot(
                    first_row, end_row, rows, 2 * face, faces_in[t, c]
                )
                value = total.astype(trace.dtype)
                if t == ITERS - 1:
                    final[c, first_row:end_row] = value
                else:
                    blocks = (end_row - first_row) // bs
                    trace[t + 1, c, first_row // bs : end_row // bs] = value.reshape(blocks, bs, width)

            if t == ITERS - 1:
                finish(0, rows)
                pltpu.make_async_copy(
                    final.at[c], result.at[:, pl.ds(c * width, width)], store_sem.at[c]
                ).start()
            else:
                finish(rows - face, rows)
                remote(t + 1, c, 0).start()
                finish(0, face)
                remote(t + 1, c, 1).start()
                finish(face, rows - face)
                send_edges(t + 1, c)
                own_term(t + 1, c)

    for t in range(ITERS):
        for c in range(CHUNKS):
            remote(t, c, 0).wait_send()
            remote(t, c, 1).wait_send()

            @pl.when(has_above)
            def _():
                remote(t, c, 2).wait_send()

            @pl.when(has_below)
            def _():
                remote(t, c, 3).wait_send()

    for c in range(CHUNKS):
        pltpu.make_async_copy(
            final.at[c], result.at[:, pl.ds(c * width, width)], store_sem.at[c]
        ).wait()


def shards(sizes, source, op_blocks, op_in, op_out, op_count, edge_up, edge_down):
    rows, columns = source.shape[2:]
    bs = op_blocks.shape[3]
    slots = op_in.shape[2]
    nb = rows // bs
    ni = nb + 2 * FX + 2 * EMAX
    width = columns // CHUNKS
    bf16 = jnp.bfloat16
    in_vmem = pl.BlockSpec(memory_space=pltpu.VMEM)
    in_smem = pl.BlockSpec(memory_space=pltpu.SMEM)
    anywhere = pl.BlockSpec(memory_space=pl.ANY)
    dense = pl.pallas_call(
        merge_kernel,
        out_shape=jax.ShapeDtypeStruct((rows, ni * bs), bf16),
        in_specs=[in_smem] * 3 + [in_vmem],
        out_specs=in_vmem,
        scratch_shapes=[
            pltpu.VMEM((slots + 1, bs, bs), jnp.float32),
            pltpu.VMEM((slots + 1, bs, bs), bf16),
            pltpu.SMEM((nb * ni + 1,), jnp.int32),
        ],
        compiler_params=pltpu.CompilerParams(vmem_limit_bytes=32 * 1024 * 1024),
    )(op_in.reshape(1, slots), op_out.reshape(1, slots), op_count, op_blocks.reshape(slots, bs, bs))
    out = pl.pallas_call(
        functools.partial(sweep_kernel, sizes),
        out_shape=jax.ShapeDtypeStruct((rows, columns), bf16),
        in_specs=[anywhere, in_vmem, in_smem, in_smem],
        out_specs=anywhere,
        scratch_shapes=[
            pltpu.VMEM((ITERS, CHUNKS, nb, bs, width), bf16),
            pltpu.VMEM((ITERS, CHUNKS, 2 * FX, bs, width), bf16),
            pltpu.VMEM((ITERS, CHUNKS, 2 * EMAX, bs, width), bf16),
            pltpu.VMEM((ITERS, CHUNKS, EMAX, bs, width), bf16),
            pltpu.VMEM((ITERS, CHUNKS, EMAX, bs, width), bf16),
            pltpu.VMEM((CHUNKS, rows, width), jnp.float32),
            pltpu.VMEM((CHUNKS, rows, width), bf16),
            pltpu.SemaphoreType.DMA((CHUNKS,)),
            pltpu.SemaphoreType.DMA((CHUNKS,)),
            pltpu.SemaphoreType.DMA((ITERS, CHUNKS, 4)),
            pltpu.SemaphoreType.DMA((ITERS, CHUNKS, 4)),
        ],
        compiler_params=pltpu.CompilerParams(
            collective_id=0, has_side_effects=True, vmem_limit_bytes=32 * 1024 * 1024
        ),
    )(source.reshape(nb, bs, columns), dense, edge_up.reshape(1, EMAX), edge_down.reshape(1, EMAX))
    return out.reshape(source.shape)


def solution(mesh):
    placed = (
        P("gx", "gy", None, None),
        P("gx", "gy", None, None),
        P("gx", "gy", None),
        P("gx", "gy", None),
        P("gx", "gy"),
        P("gx", "gy", None),
        P("gx", "gy", None),
    )
    sizes = (mesh.shape["gx"], mesh.shape["gy"])
    return jax.shard_map(
        functools.partial(shards, sizes),
        mesh=mesh,
        in_specs=placed,
        out_specs=P("gx", "gy", None, None),
        check_vma=False,
    )
```

time: 269 us -> 55.5 us (0.21); the launches traced: 264 us -> 55.4 us
  local copies, waits for them, and re-layouts: 118 us -> 3.89 us
  starting transfers between devices: 73.6 us -> 0 us
  matrix products: 63.5 us -> 0 us
  Pallas kernels: 0 us -> 50.7 us
  waiting for transfers between devices: 6.11 us -> 0 us
    ppermute x16 -> x0, starting transfers between devices: 73.6 us -> none  [the longest x8 45.2 us: from_behind(): return lax.ppermute(block, axis, route)]
    dot_general x8 -> x0, matrix products: 63.5 us -> none  [the longest x4 32.3 us: slots_term(): jnp.einsum('ekm,emr->ekr', block_now, picked, preferred_element_type=jnp....]
    pallas_call x0 -> x2, Pallas kernels: none -> 50.7 us  [the longest x1 47.8 us: shards(): pl.pallas_call(functools.partial(sweep_kernel, sizes), out_shape=jax.Shap...]
    dot_general x4 -> x0, local copies, waits for them, and re-layouts: 46.5 us -> none  [slots_term(): jnp.einsum('ekm,emr->ekr', block_now, picked, preferred_element_type=jnp....]
    gather x12 -> x0, local copies, waits for them, and re-layouts: 42.9 us -> none  [the longest x4 27.8 us: slots_term(): picked = inputs[in_now]]
    unnamed x30 -> x13, local copies, waits for them, and re-layouts: 18.5 us -> 3.89 us
    ppermute x16 -> x0, waiting for transfers between devices: 6.11 us -> none  [the longest x8 6.08 us: from_behind(): return lax.ppermute(block, axis, route)]
    convert_element_type x4 -> x0, local copies, waits for them, and re-layouts: 4.15 us -> none  [shards(): (source_blocks + totals).astype(jnp.bfloat16).reshape(row_count, columns)]
  transfers between devices with their start and end apart: 16 -> 0, of which waited for: 1 -> 0; matrix products, arithmetic and copies ran while one was open for 14% -> 0% of each run, Pallas kernels for 0% -> 0%
where the time goes in v1:
time: 55.5 us; the launch traced here: 55.4 us
  Pallas kernels  50.7 us (91%)
  local copies, waits for them, and re-layouts  3.89 us (7%)
  between operations  0.73 us (1%)
    pallas_call x1, Pallas kernels, shards(): pl.pallas_call(functools.partial(sweep_kernel, sizes), out_shape=jax.Shap...  47.8 us
    unnamed x13, local copies, waits for them, and re-layouts  3.89 us
    pallas_call x1, Pallas kernels, shards(): pl.pallas_call(merge_kernel, out_shape=jax.ShapeDtypeStruct((rows, ni * b...  2.95 us

profile of v1, /device:TPU:25, one launch (start us, length us, event | category | flops | bytes accessed | tf_op | source)
XLA Modules:
  0.0 55.4 jit_solution(9395801626488508719)
XLA Ops:
  0.0 0.0 copy-start.5
  0.0 0.0 copy-start.4
  0.7 0.0 copy-start
  0.7 1.7 %copy-done = bf16[1,1,10240,128]{3,2,1,0:T(8,128)(2,1)S(1)} copy-done((bf16[1,1,10240,128]{3,2,1,0:T(8,128)(2,1)S(1)}, bf16[1,1,10240,128]{3,2,1,0:T(8,128)(2,1)}, u32[]{:S(2)}) %copy-start) | copy-done | bytes 2621464
  2.4 0.0 copy-start.2
  2.4 0.7 %copy-done.2 = s32[1,1,80]{2,1,0:T(1,128)S(1)} copy-done((s32[1,1,80]{2,1,0:T(1,128)S(1)}, s32[1,1,80]{2,1,0:T(1,128)}, u32[]{:S(2)}) %copy-start.2) | copy-done | bytes 344
  3.1 0.0 copy-start.3
  3.1 0.7 %copy-done.3 = s32[1,1,80]{2,1,0:T(1,128)S(1)} copy-done((s32[1,1,80]{2,1,0:T(1,128)S(1)}, s32[1,1,80]{2,1,0:T(1,128)}, u32[]{:S(2)}) %copy-start.3) | copy-done | bytes 344
  3.7 0.0 copy-start.1
  3.7 2.9 %shard_map.73.dense = bf16[1280,2304]{1,0:T(8,128)(2,1)S(1)} custom-call(s32[1,80]{1,0:T(1,128)S(1)} %bitcast.10, s32[1,80]{1,0:T(1,128)S(1)} %bitcast.11, s32[1,1]{1,0:T(1,128)S(6)} %copy.9.count, bf16[80,128,128]{2,1,0:T(8,128)(2,1)S(1)} %bitcast.7), custom_call_target="tpu_custom_call" | custom-call | tf_op jit(solution)/shard_map/pallas_call | solution.py:212
  6.7 0.0 copy-done.5
  6.7 0.0 copy-done.4
  6.7 0.0 copy-done.1
  6.7 47.8 %shard_map.74 = bf16[1280,256]{1,0:T(8,128)(2,1)S(1)} custom-call(bf16[10,128,256]{2,1,0:T(8,128)(2,1)S(1)} %bitcast.9, bf16[1280,2304]{1,0:T(8,128)(2,1)S(1)} %shard_map.73.dense, s32[1,2]{1,0:T(1,128)S(1)} %bitcast.12, s32[1,2]{1,0:T(1,128)S(1)} %bitcast.13), custom_call_target="tpu_custom_call" | custom-call | tf_op jit(solution)/shard_map/pallas_call | solution.py:224
  54.5 0.8 %copy.10 = bf16[1,1,1280,256]{3,2,1,0:T(8,128)(2,1)} copy(bf16[1,1,1280,256]{3,2,1,0:T(8,128)(2,1)S(1)} %bitcast.8) | data formatting | bytes 1310720
Async XLA Ops:
  0.0 6.7 %copy-start.5 = (s32[1,1,2]{2,1,0:T(1,128)S(1)}, s32[1,1,2]{2,1,0:T(1,128)}, u32[]{:S(2)}) copy-start(s32[1,1,2]{2,1,0:T(1,128)} %param.13) | copy-start | bytes 28
  0.0 6.7 %copy-start.4 = (s32[1,1,2]{2,1,0:T(1,128)S(1)}, s32[1,1,2]{2,1,0:T(1,128)}, u32[]{:S(2)}) copy-start(s32[1,1,2]{2,1,0:T(1,128)} %param.12) | copy-start | bytes 28
  0.7 1.7 %copy-start = (bf16[1,1,10240,128]{3,2,1,0:T(8,128)(2,1)S(1)}, bf16[1,1,10240,128]{3,2,1,0:T(8,128)(2,1)}, u32[]{:S(2)}) copy-start(bf16[1,1,10240,128]{3,2,1,0:T(8,128)(2,1)} %param.8) | copy-start | bytes 7864324
  2.4 0.7 %copy-start.2 = (s32[1,1,80]{2,1,0:T(1,128)S(1)}, s32[1,1,80]{2,1,0:T(1,128)}, u32[]{:S(2)}) copy-start(s32[1,1,80]{2,1,0:T(1,128)} %param.9) | copy-start | bytes 964
  3.1 0.7 %copy-start.3 = (s32[1,1,80]{2,1,0:T(1,128)S(1)}, s32[1,1,80]{2,1,0:T(1,128)}, u32[]{:S(2)}) copy-start(s32[1,1,80]{2,1,0:T(1,128)} %param.10) | copy-start | bytes 964
  3.7 3.0 %copy-start.1 = (bf16[1,1,1280,256]{3,2,1,0:T(8,128)(2,1)S(1)}, bf16[1,1,1280,256]{3,2,1,0:T(8,128)(2,1)}, u32[]{:S(2)}) copy-start(bf16[1,1,1280,256]{3,2,1,0:T(8,128)(2,1)} %param.7) | copy-start | bytes 1966084

commit v2 on v1

v2 whole, which is shorter than its diff:
```python
import functools

import jax
import jax.numpy as jnp
from jax import lax
from jax.experimental import pallas as pl
from jax.experimental.pallas import tpu as pltpu
from jax.sharding import PartitionSpec as P

FX = 2
EMAX = 2
ITERS = 4
CHUNKS = 2
VMEM_LIMIT = 60 * 1024 * 1024
MESH = pl.DeviceIdType.MESH


LANES = 128
STRIDE = 32


def slot_table(in_row, out_row, count, table, slots, nb, ni):
    lanes = lax.broadcasted_iota(jnp.int32, (LANES, LANES), 1)
    subs = lax.broadcasted_iota(jnp.int32, (LANES, LANES), 0)
    row_ids = lax.broadcasted_iota(jnp.int32, (1, LANES), 1)
    is_own = (in_row >= FX) & (in_row < FX + nb)
    place = jnp.where(in_row < FX, in_row + nb, jnp.where(is_own, in_row - FX, in_row))
    cell_row = jnp.where(row_ids < count, place * STRIDE + out_row, 1 << 20)
    cells_t = jnp.broadcast_to(cell_row, (LANES, LANES))
    cells_s = jnp.broadcast_to(
        jnp.sum(jnp.where(lanes == subs, cells_t, 0), axis=1, keepdims=True), (LANES, LANES)
    )
    before = (cells_t < cells_s) | ((cells_t == cells_s) & (lanes < subs))
    rank = jnp.broadcast_to(
        jnp.sum(jnp.where(before, 1, 0), axis=1, keepdims=True), (LANES, LANES)
    )
    perm = jnp.sum(jnp.where(rank == lanes, subs, 0), axis=0, keepdims=True)
    here = jnp.sum(jnp.where(rank == lanes, cells_s, 0), axis=0, keepdims=True)
    previous = jnp.sum(jnp.where(rank + 1 == lanes, cells_s, 0), axis=0, keepdims=True)
    table[0:1, :] = jnp.minimum(perm, slots - 1)
    table[1:2, :] = jnp.where((row_ids > 0) & (here == previous), 1, 0)
    for part in range(-(-ni * STRIDE // LANES)):
        wanted = lanes + part * LANES
        upto = jnp.sum(jnp.where(cells_s <= wanted, 1, 0), axis=0, keepdims=True)
        equal = jnp.sum(jnp.where(cells_s == wanted, 1, 0), axis=0, keepdims=True)
        table[2 + part : 3 + part, :] = jnp.where(equal > 0, upto - 1, slots)


def sweep_kernel(
    sizes, source, blocks, ops_in, ops_out, count, ups, downs, result,
    raw, trace, faces_in, edges_in, up_pick, down_pick, own_sum, final,
    ops, merged, dense, in_row, out_row, table, places,
    load_sem, table_sem, store_sem, send_sem, recv_sem,
):
    n_gx, n_gy = sizes
    nb, width, bs = trace.shape[2:]
    slots, ni = blocks.shape[0], dense.shape[0] // bs
    gx, gy = lax.axis_index("gx"), lax.axis_index("gy")
    right = (lax.rem(gx + 1, n_gx), gy)
    left = (lax.rem(gx + n_gx - 1, n_gx), gy)
    above = (gx, lax.rem(gy + 1, n_gy))
    below = (gx, lax.rem(gy + n_gy - 1, n_gy))
    has_above, has_below = gy < n_gy - 1, gy > 0

    barrier = pltpu.get_barrier_semaphore()
    for place in (right, left):
        pl.semaphore_signal(barrier, inc=1, device_id=place, device_id_type=MESH)

    @pl.when(has_above)
    def _():
        pl.semaphore_signal(barrier, inc=1, device_id=above, device_id_type=MESH)

    @pl.when(has_below)
    def _():
        pl.semaphore_signal(barrier, inc=1, device_id=below, device_id_type=MESH)

    loads = [
        pltpu.make_async_copy(
            source.at[:, :, pl.ds(c * width, width)], raw.at[c], load_sem.at[c]
        )
        for c in range(CHUNKS)
    ]
    ops_load = pltpu.make_async_copy(blocks, ops, load_sem.at[CHUNKS])
    for copy in loads + [ops_load]:
        copy.start()

    in_row[...] = jnp.zeros_like(in_row)
    out_row[...] = jnp.zeros_like(out_row)
    in_row[:, 0:slots] = ops_in[...]
    out_row[:, 0:slots] = ops_out[...]
    slot_table(in_row[...], out_row[...], count[0, 0], table, slots, nb, ni)
    table_copy = pltpu.make_async_copy(table, places, table_sem)
    table_copy.start()

    @pl.when(jnp.logical_not(has_below))
    def _():
        edges_in[:, :, 0:EMAX] = jnp.zeros((ITERS, CHUNKS, EMAX, width, bs), edges_in.dtype)

    @pl.when(jnp.logical_not(has_above))
    def _():
        edges_in[:, :, EMAX:] = jnp.zeros((ITERS, CHUNKS, EMAX, width, bs), edges_in.dtype)

    def remote(t, c, which):
        src, dst, place = (
            (trace.at[t, c, pl.ds(nb - FX, FX)], faces_in.at[t, c, pl.ds(0, FX)], right),
            (trace.at[t, c, pl.ds(0, FX)], faces_in.at[t, c, pl.ds(FX, FX)], left),
            (up_pick.at[t, c], edges_in.at[t, c, pl.ds(0, EMAX)], above),
            (down_pick.at[t, c], edges_in.at[t, c, pl.ds(EMAX, EMAX)], below),
        )[which]
        return pltpu.make_async_remote_copy(
            src_ref=src,
            dst_ref=dst,
            send_sem=send_sem.at[t, c, which],
            recv_sem=recv_sem.at[t, c, which],
            device_id=place,
            device_id_type=MESH,
        )

    def send_edges(t, c):
        @pl.when(has_above)
        def _():
            for k in range(EMAX):
                up_pick[t, c, k] = trace[t, c, ups[0, k]]
            remote(t, c, 2).start()

        @pl.when(has_below)
        def _():
            for k in range(EMAX):
                down_pick[t, c, k] = trace[t, c, downs[0, k]]
            remote(t, c, 3).start()

    def side_by_side(ref, t, c, count):
        return jnp.concatenate([ref[t, c, j] for j in range(count)], axis=1)

    def dot(inputs, first, end, first_out, end_out):
        return jnp.dot(
            inputs,
            dense[first * bs : end * bs, first_out * bs : end_out * bs],
            preferred_element_type=jnp.float32,
        )

    def own_term(t, c):
        terms = side_by_side(trace, 0, c, nb).astype(jnp.float32)
        own_sum[c] = terms + dot(side_by_side(trace, t, c, nb), 0, nb, 0, nb)

    waited = False
    for c in range(CHUNKS):
        loads[c].wait()
        for j in range(nb):
            trace[0, c, j] = raw[c, j].astype(jnp.float32).T.astype(trace.dtype)
        if not waited:
            pl.semaphore_wait(
                barrier, 2 + has_above.astype(jnp.int32) + has_below.astype(jnp.int32)
            )
            waited = True
        remote(0, c, 0).start()
        remote(0, c, 1).start()
        send_edges(0, c)

    table_copy.wait()
    ops_load.wait()
    merged[slots] = jnp.zeros((bs, bs), merged.dtype)

    def merge(p, total):
        total = jnp.where(places[1, p] > 0, total, 0.0) + ops[places[0, p]].astype(jnp.float32)
        merged[p] = total.T.astype(merged.dtype)
        return total

    lax.fori_loop(0, slots, merge, jnp.zeros((bs, bs), jnp.float32), unroll=4)
    for i in range(ni):
        for j in range(nb):
            cell = i * STRIDE + j
            dense[i * bs : (i + 1) * bs, j * bs : (j + 1) * bs] = merged[
                places[2 + cell // LANES, cell % LANES]
            ]
    for c in range(CHUNKS):
        own_term(0, c)

    for t in range(ITERS):
        for c in range(CHUNKS):
            @pl.when(has_below)
            def _():
                remote(t, c, 2).wait_recv()

            @pl.when(has_above)
            def _():
                remote(t, c, 3).wait_recv()

            own_sum[c] += dot(
                side_by_side(edges_in, t, c, 2 * EMAX), nb + 2 * FX, ni, 0, nb
            )
            remote(t, c, 0).wait_recv()
            remote(t, c, 1).wait_recv()

            faces = side_by_side(faces_in, t, c, 2 * FX)

            def finish(first, end):
                total = own_sum[c, :, first * bs : end * bs] + dot(
                    faces, nb, nb + 2 * FX, first, end
                )
                if t == ITERS - 1:
                    final[c] = total.T.astype(final.dtype)
                else:
                    for j in range(first, end):
                        trace[t + 1, c, j] = total[:, (j - first) * bs : (j - first + 1) * bs].astype(
                            trace.dtype
                        )

            if t == ITERS - 1:
                finish(0, nb)
                pltpu.make_async_copy(
                    final.at[c], result.at[:, pl.ds(c * width, width)], store_sem.at[c]
                ).start()
            else:
                finish(nb - FX, nb)
                remote(t + 1, c, 0).start()
                finish(0, FX)
                remote(t + 1, c, 1).start()
                finish(FX, nb - FX)
                send_edges(t + 1, c)
                own_term(t + 1, c)

    for t in range(ITERS):
        for c in range(CHUNKS):
            remote(t, c, 0).wait_send()
            remote(t, c, 1).wait_send()

            @pl.when(has_above)
            def _():
                remote(t, c, 2).wait_send()

            @pl.when(has_below)
            def _():
                remote(t, c, 3).wait_send()

    for c in range(CHUNKS):
        pltpu.make_async_copy(
            final.at[c], result.at[:, pl.ds(c * width, width)], store_sem.at[c]
        ).wait()


def shards(sizes, source, op_blocks, op_in, op_out, op_count, edge_up, edge_down):
    rows, columns = source.shape[2:]
    bs = op_blocks.shape[3]
    slots = op_in.shape[2]
    nb = rows // bs
    ni = nb + 2 * FX + 2 * EMAX
    width = columns // CHUNKS
    bf16 = jnp.bfloat16
    in_vmem = pl.BlockSpec(memory_space=pltpu.VMEM)
    in_smem = pl.BlockSpec(memory_space=pltpu.SMEM)
    anywhere = pl.BlockSpec(memory_space=pl.ANY)
    out = pl.pallas_call(
        functools.partial(sweep_kernel, sizes),
        out_shape=jax.ShapeDtypeStruct((rows, columns), bf16),
        in_specs=[anywhere] * 2 + [in_vmem] * 2 + [in_smem] * 3,
        out_specs=anywhere,
        scratch_shapes=[
            pltpu.VMEM((CHUNKS, nb, bs, width), bf16),
            pltpu.VMEM((ITERS, CHUNKS, nb, width, bs), bf16),
            pltpu.VMEM((ITERS, CHUNKS, 2 * FX, width, bs), bf16),
            pltpu.VMEM((ITERS, CHUNKS, 2 * EMAX, width, bs), bf16),
            pltpu.VMEM((ITERS, CHUNKS, EMAX, width, bs), bf16),
            pltpu.VMEM((ITERS, CHUNKS, EMAX, width, bs), bf16),
            pltpu.VMEM((CHUNKS, width, rows), jnp.float32),
            pltpu.VMEM((CHUNKS, rows, width), bf16),
            pltpu.VMEM((slots, bs, bs), bf16),
            pltpu.VMEM((slots + 1, bs, bs), bf16),
            pltpu.VMEM((ni * bs, rows), bf16),
            pltpu.VMEM((1, LANES), jnp.int32),
            pltpu.VMEM((1, LANES), jnp.int32),
            pltpu.VMEM((8, LANES), jnp.int32),
            pltpu.SMEM((8, LANES), jnp.int32),
            pltpu.SemaphoreType.DMA((CHUNKS + 1,)),
            pltpu.SemaphoreType.DMA,
            pltpu.SemaphoreType.DMA((CHUNKS,)),
            pltpu.SemaphoreType.DMA((ITERS, CHUNKS, 4)),
            pltpu.SemaphoreType.DMA((ITERS, CHUNKS, 4)),
        ],
        compiler_params=pltpu.CompilerParams(
            collective_id=0, has_side_effects=True, vmem_limit_bytes=VMEM_LIMIT
        ),
    )(
        source.reshape(nb, bs, columns),
        op_blocks.reshape(slots, bs, bs),
        op_in.reshape(1, slots),
        op_out.reshape(1, slots),
        op_count,
        edge_up.reshape(1, EMAX),
        edge_down.reshape(1, EMAX),
    )
    return out.reshape(source.shape)


def solution(mesh):
    placed = (
        P("gx", "gy", None, None),
        P("gx", "gy", None, None),
        P("gx", "gy", None),
        P("gx", "gy", None),
        P("gx", "gy"),
        P("gx", "gy", None),
        P("gx", "gy", None),
    )
    sizes = (mesh.shape["gx"], mesh.shape["gy"])
    return jax.shard_map(
        functools.partial(shards, sizes),
        mesh=mesh,
        in_specs=placed,
        out_specs=P("gx", "gy", None, None),
        check_vma=False,
    )
```

time: 55.5 us -> 50.4 us (0.908)
  Pallas kernels: 50.7 us -> 47.6 us
  local copies, waits for them, and re-layouts: 3.89 us -> 1.97 us
    pallas_call x1 -> x0, Pallas kernels: 2.95 us -> none  [shards(): pl.pallas_call(merge_kernel, out_shape=jax.ShapeDtypeStruct((rows, ni * b...]
    unnamed x13 -> x1, local copies, waits for them, and re-layouts: 3.89 us -> 1.97 us
where the time goes in v2:
time: 50.4 us; the launch traced here: 50.3 us
  Pallas kernels  47.6 us (94%)
  local copies, waits for them, and re-layouts  1.97 us (4%)
  between operations  0.66 us (1%)
    pallas_call x1, Pallas kernels, shards(): pl.pallas_call(functools.partial(sweep_kernel, sizes), out_shape=jax.Shap...  47.6 us
    unnamed x1, local copies, waits for them, and re-layouts  1.97 us

profile of v2, /device:TPU:25, one launch (start us, length us, event | category | flops | bytes accessed | tf_op | source)
XLA Modules:
  0.0 50.3 jit_solution(15479915626136842963)
XLA Ops:
  0.7 47.6 %shard_map.73 = bf16[1280,256]{1,0:T(8,128)(2,1)} custom-call(bf16[10,128,256]{2,1,0:T(8,128)(2,1)} %bitcast.9, bf16[80,128,128]{2,1,0:T(8,128)(2,1)} %bitcast.7, s32[1,80]{1,0:T(1,128)} %bitcast.10, s32[1,80]{1,0:T(1,128)} %bitcast.11, s32[1,1]{1,0:T(1,128)S(6)} %copy.9.count, s32[1,2]{1,0:T(1,128)} %bitcast.12, s32[1,2]{1,0:T(1,128)} %bitcast.13), custom_call_target="tpu_custom_call" | custom-call | tf_op jit(solution)/shard_map/pallas_call | solution.py:253
  48.3 2.0 %copy.10 = bf16[1,1,1280,256]{3,2,1,0:T(8,128)(2,1)} copy(bf16[1,1,1280,256]{3,2,1,0:T(8,128)(2,1)} %bitcast.8) | data formatting | bytes 1310720

commit v3 on v2

--- a/solution.py
+++ b/solution.py
@@ -11,7 +11,7 @@
 EMAX = 2
 ITERS = 4
 CHUNKS = 2
-VMEM_LIMIT = 60 * 1024 * 1024
+VMEM_LIMIT = 58 * 1024 * 1024
 MESH = pl.DeviceIdType.MESH
 
 
@@ -47,10 +47,10 @@
 
 
 def sweep_kernel(
-    sizes, source, blocks, ops_in, ops_out, count, ups, downs, result,
-    raw, trace, faces_in, edges_in, up_pick, down_pick, own_sum, final,
-    ops, merged, dense, in_row, out_row, table, places,
-    load_sem, table_sem, store_sem, send_sem, recv_sem,
+    sizes, source, blocks, ops_in, ops_out, count, ups_in, downs_in, result,
+    raw, trace, faces_in, edges_in, up_pick, down_pick, own_sum,
+    ops, merged, dense, in_list, out_list, in_row, out_row, table, places, ups, downs,
+    load_sem, small_sem, table_sem, send_sem, recv_sem,
 ):
     n_gx, n_gy = sizes
     nb, width, bs = trace.shape[2:]
@@ -81,13 +81,19 @@
         for c in range(CHUNKS)
     ]
     ops_load = pltpu.make_async_copy(blocks, ops, load_sem.at[CHUNKS])
-    for copy in loads + [ops_load]:
+    pairs = ((ops_in, in_list), (ops_out, out_list), (ups_in, ups), (downs_in, downs))
+    small = [
+        pltpu.make_async_copy(src, dst, small_sem.at[k]) for k, (src, dst) in enumerate(pairs)
+    ]
+    for copy in loads + small:
         copy.start()
 
     in_row[...] = jnp.zeros_like(in_row)
     out_row[...] = jnp.zeros_like(out_row)
-    in_row[:, 0:slots] = ops_in[...]
-    out_row[:, 0:slots] = ops_out[...]
+    for copy in small:
+        copy.wait()
+    in_row[:, 0:slots] = in_list[...]
+    out_row[:, 0:slots] = out_list[...]
     slot_table(in_row[...], out_row[...], count[0, 0], table, slots, nb, ni)
     table_copy = pltpu.make_async_copy(table, places, table_sem)
     table_copy.start()
@@ -143,19 +149,19 @@
         terms = side_by_side(trace, 0, c, nb).astype(jnp.float32)
         own_sum[c] = terms + dot(side_by_side(trace, t, c, nb), 0, nb, 0, nb)
 
-    waited = False
     for c in range(CHUNKS):
         loads[c].wait()
-        for j in range(nb):
+        for j in (*range(nb - FX, nb), *range(nb - FX)):
             trace[0, c, j] = raw[c, j].astype(jnp.float32).T.astype(trace.dtype)
-        if not waited:
-            pl.semaphore_wait(
-                barrier, 2 + has_above.astype(jnp.int32) + has_below.astype(jnp.int32)
-            )
-            waited = True
-        remote(0, c, 0).start()
-        remote(0, c, 1).start()
+            if j == FX - 1:
+                if c == 0:
+                    pl.semaphore_wait(
+                        barrier, 2 + has_above.astype(jnp.int32) + has_below.astype(jnp.int32)
+                    )
+                remote(0, c, 0).start()
+                remote(0, c, 1).start()
         send_edges(0, c)
+    ops_load.start()
 
     table_copy.wait()
     ops_load.wait()
@@ -199,7 +205,7 @@
                     faces, nb, nb + 2 * FX, first, end
                 )
                 if t == ITERS - 1:
-                    final[c] = total.T.astype(final.dtype)
+                    result[:, c * width : (c + 1) * width] = total.T.astype(result.dtype)
                 else:
                     for j in range(first, end):
                         trace[t + 1, c, j] = total[:, (j - first) * bs : (j - first + 1) * bs].astype(
@@ -208,9 +214,6 @@
 
             if t == ITERS - 1:
                 finish(0, nb)
-                pltpu.make_async_copy(
-                    final.at[c], result.at[:, pl.ds(c * width, width)], store_sem.at[c]
-                ).start()
             else:
                 finish(nb - FX, nb)
                 remote(t + 1, c, 0).start()
@@ -233,11 +236,6 @@
             def _():
                 remote(t, c, 3).wait_send()
 
-    for c in range(CHUNKS):
-        pltpu.make_async_copy(
-            final.at[c], result.at[:, pl.ds(c * width, width)], store_sem.at[c]
-        ).wait()
-
 
 def shards(sizes, source, op_blocks, op_in, op_out, op_count, edge_up, edge_down):
     rows, columns = source.shape[2:]
@@ -247,14 +245,14 @@
     ni = nb + 2 * FX + 2 * EMAX
     width = columns // CHUNKS
     bf16 = jnp.bfloat16
+    in_smem = pl.BlockSpec(memory_space=pltpu.SMEM)
     in_vmem = pl.BlockSpec(memory_space=pltpu.VMEM)
-    in_smem = pl.BlockSpec(memory_space=pltpu.SMEM)
     anywhere = pl.BlockSpec(memory_space=pl.ANY)
     out = pl.pallas_call(
         functools.partial(sweep_kernel, sizes),
-        out_shape=jax.ShapeDtypeStruct((rows, columns), bf16),
-        in_specs=[anywhere] * 2 + [in_vmem] * 2 + [in_smem] * 3,
-        out_specs=anywhere,
+        out_shape=pltpu.VMEM((rows, columns), bf16),
+        in_specs=[anywhere] * 4 + [in_smem] + [anywhere] * 2,
+        out_specs=in_vmem,
         scratch_shapes=[
             pltpu.VMEM((CHUNKS, nb, bs, width), bf16),
             pltpu.VMEM((ITERS, CHUNKS, nb, width, bs), bf16),
@@ -263,17 +261,20 @@
             pltpu.VMEM((ITERS, CHUNKS, EMAX, width, bs), bf16),
             pltpu.VMEM((ITERS, CHUNKS, EMAX, width, bs), bf16),
             pltpu.VMEM((CHUNKS, width, rows), jnp.float32),
-            pltpu.VMEM((CHUNKS, rows, width), bf16),
             pltpu.VMEM((slots, bs, bs), bf16),
             pltpu.VMEM((slots + 1, bs, bs), bf16),
             pltpu.VMEM((ni * bs, rows), bf16),
+            pltpu.VMEM((1, slots), jnp.int32),
+            pltpu.VMEM((1, slots), jnp.int32),
             pltpu.VMEM((1, LANES), jnp.int32),
             pltpu.VMEM((1, LANES), jnp.int32),
             pltpu.VMEM((8, LANES), jnp.int32),
             pltpu.SMEM((8, LANES), jnp.int32),
+            pltpu.SMEM((1, EMAX), jnp.int32),
+            pltpu.SMEM((1, EMAX), jnp.int32),
             pltpu.SemaphoreType.DMA((CHUNKS + 1,)),
+            pltpu.SemaphoreType.DMA((4,)),
             pltpu.SemaphoreType.DMA,
-            pltpu.SemaphoreType.DMA((CHUNKS,)),
             pltpu.SemaphoreType.DMA((ITERS, CHUNKS, 4)),
             pltpu.SemaphoreType.DMA((ITERS, CHUNKS, 4)),
         ],

time: 50.4 us -> 47.6 us (0.944)
  Pallas kernels: 47.6 us -> 45.9 us
  local copies, waits for them, and re-layouts: 1.97 us -> 0.84 us
    pallas_call x1, Pallas kernels: 47.6 us -> 45.9 us  [shards(): pl.pallas_call(functools.partial(sweep_kernel, sizes), out_shape=pltpu.VM...]
    unnamed x1, local copies, waits for them, and re-layouts: 1.97 us -> 0.84 us
where the time goes in v3:
time: 47.6 us; the launch traced here: 47.4 us
  Pallas kernels  45.9 us (96%)
  local copies, waits for them, and re-layouts  0.84 us (2%)
  between operations  0.66 us (1%)
    pallas_call x1, Pallas kernels, shards(): pl.pallas_call(functools.partial(sweep_kernel, sizes), out_shape=pltpu.VM...  45.9 us

profile of v3, /device:TPU:25, one launch (start us, length us, event | category | flops | bytes accessed | tf_op | source)
XLA Modules:
  0.0 47.4 jit_solution(2649918938337860961)
XLA Ops:
  0.7 45.9 %shard_map.73 = bf16[1280,256]{1,0:T(8,128)(2,1)S(1)} custom-call(bf16[10,128,256]{2,1,0:T(8,128)(2,1)} %bitcast.9, bf16[80,128,128]{2,1,0:T(8,128)(2,1)} %bitcast.8, s32[1,80]{1,0:T(1,128)} %bitcast.10, s32[1,80]{1,0:T(1,128)} %bitcast.11, s32[1,1]{1,0:T(1,128)S(6)} %copy.10.count, s32[1,2]{1,0:T(1,128)} %bitcast.12, s32[1,2]{1,0:T(1,128)} %bitcast.13), custom_call_target="tpu_custom_call" | custom-call | tf_op jit(solution)/shard_map/pallas_call | solution.py:251
  46.6 0.8 %copy.9 = bf16[1,1,1280,256]{3,2,1,0:T(8,128)(2,1)} copy(bf16[1,1,1280,256]{3,2,1,0:T(8,128)(2,1)S(1)} %bitcast.7) | data formatting | bytes 1310720

commit v4 on v3

--- a/solution.py
+++ b/solution.py
@@ -12,6 +12,7 @@
 ITERS = 4
 CHUNKS = 2
 VMEM_LIMIT = 58 * 1024 * 1024
+RELAYS = {(0, 1): 0, (1, 0): 2, (1, 1): 4}
 MESH = pl.DeviceIdType.MESH
 
 
@@ -48,9 +49,10 @@
 
 def sweep_kernel(
     sizes, source, blocks, ops_in, ops_out, count, ups_in, downs_in, result,
-    raw, trace, faces_in, edges_in, up_pick, down_pick, own_sum,
+    raw, trace, relay_in, faces_in, edges_in, up_pick, down_pick, own_sum,
     ops, merged, dense, in_list, out_list, in_row, out_row, table, places, ups, downs,
     load_sem, small_sem, table_sem, send_sem, recv_sem,
+    cross_send, cross_recv, relay_send, relay_recv,
 ):
     n_gx, n_gy = sizes
     nb, width, bs = trace.shape[2:]
@@ -62,6 +64,19 @@
     below = (gx, lax.rem(gy + n_gy - 1, n_gy))
     has_above, has_below = gy < n_gy - 1, gy > 0
 
+    middle = n_gy // 2
+    low, high = gy == middle - 1, gy == middle
+    up_relays = sorted(RELAYS.values())
+    down_relays = [n_gy - 1 - relay for relay in up_relays]
+    is_relay = functools.reduce(jnp.logical_or, [gy == r for r in up_relays + down_relays])
+    greeted = (
+        2
+        + has_above.astype(jnp.int32)
+        + has_below.astype(jnp.int32)
+        + 2 * is_relay.astype(jnp.int32)
+        + 2 * len(RELAYS) * jnp.logical_or(low, high).astype(jnp.int32)
+    )
+
     barrier = pltpu.get_barrier_semaphore()
     for place in (right, left):
         pl.semaphore_signal(barrier, inc=1, device_id=place, device_id_type=MESH)
@@ -73,6 +88,16 @@
     @pl.when(has_below)
     def _():
         pl.semaphore_signal(barrier, inc=1, device_id=below, device_id_type=MESH)
+
+    @pl.when(is_relay)
+    def _():
+        for end in (middle - 1, middle):
+            pl.semaphore_signal(barrier, inc=1, device_id=(gx, end), device_id_type=MESH)
+
+    @pl.when(jnp.logical_or(low, high))
+    def _():
+        for relay in up_relays + down_relays:
+            pl.semaphore_signal(barrier, inc=1, device_id=(gx, relay), device_id_type=MESH)
 
     loads = [
         pltpu.make_async_copy(
@@ -122,18 +147,70 @@
             device_id_type=MESH,
         )
 
+    ways = (
+        (low, high, middle, up_pick, 0, lambda relay: relay),
+        (high, low, middle - 1, down_pick, EMAX, lambda relay: n_gy - 1 - relay),
+    )
+
+    def crossing(way, t, c, k):
+        _, _, end, pick, first, side = way
+        relay = side(RELAYS[c, k]) if (c, k) in RELAYS else None
+        return pltpu.make_async_remote_copy(
+            src_ref=pick.at[t, c, k],
+            dst_ref=edges_in.at[t, c, first + k] if relay is None else relay_in.at[t, c, k],
+            send_sem=cross_send.at[t, c, k],
+            recv_sem=cross_recv.at[t, c, k] if relay is None else relay_recv.at[t, c, k],
+            device_id=(gx, end if relay is None else relay),
+            device_id_type=MESH,
+        )
+
+    def onward(way, t, c, k):
+        _, _, end, _, first, _ = way
+        return pltpu.make_async_remote_copy(
+            src_ref=relay_in.at[t, c, k],
+            dst_ref=edges_in.at[t, c, first + k],
+            send_sem=relay_send.at[t, c, k],
+            recv_sem=cross_recv.at[t, c, k],
+            device_id=(gx, end),
+            device_id_type=MESH,
+        )
+
+    def forward(t, c):
+        for (chunk, k), relay in RELAYS.items():
+            if chunk == c:
+                for way in ways:
+                    @pl.when(gy == way[5](relay))
+                    def _():
+                        crossing(way, t, c, k).wait_recv()
+                        onward(way, t, c, k).start()
+
+    plain_above = jnp.logical_and(has_above, jnp.logical_not(low))
+    plain_below = jnp.logical_and(has_below, jnp.logical_not(high))
+
     def send_edges(t, c):
         @pl.when(has_above)
         def _():
             for k in range(EMAX):
                 up_pick[t, c, k] = trace[t, c, ups[0, k]]
-            remote(t, c, 2).start()
 
         @pl.when(has_below)
         def _():
             for k in range(EMAX):
                 down_pick[t, c, k] = trace[t, c, downs[0, k]]
+
+        @pl.when(plain_above)
+        def _():
+            remote(t, c, 2).start()
+
+        @pl.when(plain_below)
+        def _():
             remote(t, c, 3).start()
+
+        for way in ways:
+            @pl.when(way[0])
+            def _():
+                for k in range(EMAX):
+                    crossing(way, t, c, k).start()
 
     def side_by_side(ref, t, c, count):
         return jnp.concatenate([ref[t, c, j] for j in range(count)], axis=1)
@@ -155,9 +232,7 @@
             trace[0, c, j] = raw[c, j].astype(jnp.float32).T.astype(trace.dtype)
             if j == FX - 1:
                 if c == 0:
-                    pl.semaphore_wait(
-                        barrier, 2 + has_above.astype(jnp.int32) + has_below.astype(jnp.int32)
-                    )
+                    pl.semaphore_wait(barrier, greeted)
                 remote(0, c, 0).start()
                 remote(0, c, 1).start()
         send_edges(0, c)
@@ -180,17 +255,25 @@
                 places[2 + cell // LANES, cell % LANES]
             ]
     for c in range(CHUNKS):
+        forward(0, c)
+    for c in range(CHUNKS):
         own_term(0, c)
 
     for t in range(ITERS):
         for c in range(CHUNKS):
-            @pl.when(has_below)
+            @pl.when(plain_below)
             def _():
                 remote(t, c, 2).wait_recv()
 
-            @pl.when(has_above)
+            @pl.when(plain_above)
             def _():
                 remote(t, c, 3).wait_recv()
+
+            for way in ways:
+                @pl.when(way[1])
+                def _():
+                    for k in range(EMAX):
+                        onward(way, t, c, k).wait_recv()
 
             own_sum[c] += dot(
                 side_by_side(edges_in, t, c, 2 * EMAX), nb + 2 * FX, ni, 0, nb
@@ -214,6 +297,8 @@
 
             if t == ITERS - 1:
                 finish(0, nb)
+                if c == 0:
+                    forward(t, 1)
             else:
                 finish(nb - FX, nb)
                 remote(t + 1, c, 0).start()
@@ -221,6 +306,10 @@
                 remote(t + 1, c, 1).start()
                 finish(FX, nb - FX)
                 send_edges(t + 1, c)
+                if c == 1:
+                    forward(t + 1, 0)
+                elif t > 0:
+                    forward(t, 1)
                 own_term(t + 1, c)
 
     for t in range(ITERS):
@@ -228,13 +317,25 @@
             remote(t, c, 0).wait_send()
             remote(t, c, 1).wait_send()
 
-            @pl.when(has_above)
+            @pl.when(plain_above)
             def _():
                 remote(t, c, 2).wait_send()
 
-            @pl.when(has_below)
+            @pl.when(plain_below)
             def _():
                 remote(t, c, 3).wait_send()
+
+            for way in ways:
+                @pl.when(way[0])
+                def _():
+                    for k in range(EMAX):
+                        crossing(way, t, c, k).wait_send()
+
+                for k in range(EMAX):
+                    if (c, k) in RELAYS:
+                        @pl.when(gy == way[5](RELAYS[c, k]))
+                        def _():
+                            onward(way, t, c, k).wait_send()
 
 
 def shards(sizes, source, op_blocks, op_in, op_out, op_count, edge_up, edge_down):
@@ -256,6 +357,7 @@
         scratch_shapes=[
             pltpu.VMEM((CHUNKS, nb, bs, width), bf16),
             pltpu.VMEM((ITERS, CHUNKS, nb, width, bs), bf16),
+            pltpu.VMEM((ITERS, CHUNKS, EMAX, width, bs), bf16),
             pltpu.VMEM((ITERS, CHUNKS, 2 * FX, width, bs), bf16),
             pltpu.VMEM((ITERS, CHUNKS, 2 * EMAX, width, bs), bf16),
             pltpu.VMEM((ITERS, CHUNKS, EMAX, width, bs), bf16),
@@ -277,6 +379,10 @@
             pltpu.SemaphoreType.DMA,
             pltpu.SemaphoreType.DMA((ITERS, CHUNKS, 4)),
             pltpu.SemaphoreType.DMA((ITERS, CHUNKS, 4)),
+            pltpu.SemaphoreType.DMA((ITERS, CHUNKS, EMAX)),
+            pltpu.SemaphoreType.DMA((ITERS, CHUNKS, EMAX)),
+            pltpu.SemaphoreType.DMA((ITERS, CHUNKS, EMAX)),
+            pltpu.SemaphoreType.DMA((ITERS, CHUNKS, EMAX)),
         ],
         compiler_params=pltpu.CompilerParams(
             collective_id=0, has_side_effects=True, vmem_limit_bytes=VMEM_LIMIT

time: 47.6 us -> 52.9 us (1.11)
  the two profiles are of different devices: /device:TPU:25 before, /device:TPU:2 now
where the time goes in v4:
time: 52.9 us; the launch traced here: 52.7 us
  Pallas kernels  51.2 us (97%)
  local copies, waits for them, and re-layouts  0.84 us (2%)
  between operations  0.66 us (1%)
    pallas_call x1, Pallas kernels, shards(): pl.pallas_call(functools.partial(sweep_kernel, sizes), out_shape=pltpu.VM...  51.2 us

profile of v4, /device:TPU:2, one launch (start us, length us, event | category | flops | bytes accessed | tf_op | source)
XLA Modules:
  0.0 52.7 jit_solution(10083750604809858321)
XLA Ops:
  0.7 51.2 %shard_map.73 = bf16[1280,256]{1,0:T(8,128)(2,1)S(1)} custom-call(bf16[10,128,256]{2,1,0:T(8,128)(2,1)} %bitcast.9, bf16[80,128,128]{2,1,0:T(8,128)(2,1)} %bitcast.8, s32[1,80]{1,0:T(1,128)} %bitcast.10, s32[1,80]{1,0:T(1,128)} %bitcast.11, s32[1,1]{1,0:T(1,128)S(6)} %copy.10.count, s32[1,2]{1,0:T(1,128)} %bitcast.12, s32[1,2]{1,0:T(1,128)} %bitcast.13), custom_call_target="tpu_custom_call" | custom-call | tf_op jit(solution)/shard_map/pallas_call | solution.py:352
  51.8 0.8 %copy.9 = bf16[1,1,1280,256]{3,2,1,0:T(8,128)(2,1)} copy(bf16[1,1,1280,256]{3,2,1,0:T(8,128)(2,1)S(1)} %bitcast.7) | data formatting | bytes 1310720

commit v5 on v4

--- a/solution.py
+++ b/solution.py
@@ -12,7 +12,7 @@
 ITERS = 4
 CHUNKS = 2
 VMEM_LIMIT = 58 * 1024 * 1024
-RELAYS = {(0, 1): 0, (1, 0): 2, (1, 1): 4}
+RELAYS = {(0, 1): 0, (1, 1): 0}
 MESH = pl.DeviceIdType.MESH
 
 
@@ -66,7 +66,7 @@
 
     middle = n_gy // 2
     low, high = gy == middle - 1, gy == middle
-    up_relays = sorted(RELAYS.values())
+    up_relays = sorted(set(RELAYS.values()))
     down_relays = [n_gy - 1 - relay for relay in up_relays]
     is_relay = functools.reduce(jnp.logical_or, [gy == r for r in up_relays + down_relays])
     greeted = (
@@ -74,7 +74,7 @@
         + has_above.astype(jnp.int32)
         + has_below.astype(jnp.int32)
         + 2 * is_relay.astype(jnp.int32)
-        + 2 * len(RELAYS) * jnp.logical_or(low, high).astype(jnp.int32)
+        + 2 * len(up_relays) * jnp.logical_or(low, high).astype(jnp.int32)
     )
 
     barrier = pltpu.get_barrier_semaphore()
@@ -248,14 +248,14 @@
         return total
 
     lax.fori_loop(0, slots, merge, jnp.zeros((bs, bs), jnp.float32), unroll=4)
+    for c in range(CHUNKS):
+        forward(0, c)
     for i in range(ni):
         for j in range(nb):
             cell = i * STRIDE + j
             dense[i * bs : (i + 1) * bs, j * bs : (j + 1) * bs] = merged[
                 places[2 + cell // LANES, cell % LANES]
             ]
-    for c in range(CHUNKS):
-        forward(0, c)
     for c in range(CHUNKS):
         own_term(0, c)
 
@@ -297,8 +297,6 @@
 
             if t == ITERS - 1:
                 finish(0, nb)
-                if c == 0:
-                    forward(t, 1)
             else:
                 finish(nb - FX, nb)
                 remote(t + 1, c, 0).start()
@@ -306,11 +304,8 @@
                 remote(t + 1, c, 1).start()
                 finish(FX, nb - FX)
                 send_edges(t + 1, c)
-                if c == 1:
-                    forward(t + 1, 0)
-                elif t > 0:
-                    forward(t, 1)
                 own_term(t + 1, c)
+                forward(t + 1, c)
 
     for t in range(ITERS):
         for c in range(CHUNKS):

time: 52.9 us -> 49.1 us (0.928)
  the two profiles are of different devices: /device:TPU:2 before, /device:TPU:25 now
where the time goes in v5:
time: 49.1 us; the launch traced here: 48.5 us
  Pallas kernels  47 us (96%)
  local copies, waits for them, and re-layouts  0.84 us (2%)
  between operations  0.66 us (1%)
    pallas_call x1, Pallas kernels, shards(): pl.pallas_call(functools.partial(sweep_kernel, sizes), out_shape=pltpu.VM...  47 us

profile of v5, /device:TPU:25, one launch (start us, length us, event | category | flops | bytes accessed | tf_op | source)
XLA Modules:
  0.0 48.5 jit_solution(7841446372137749239)
XLA Ops:
  0.7 47.0 %shard_map.73 = bf16[1280,256]{1,0:T(8,128)(2,1)S(1)} custom-call(bf16[10,128,256]{2,1,0:T(8,128)(2,1)} %bitcast.9, bf16[80,128,128]{2,1,0:T(8,128)(2,1)} %bitcast.8, s32[1,80]{1,0:T(1,128)} %bitcast.10, s32[1,80]{1,0:T(1,128)} %bitcast.11, s32[1,1]{1,0:T(1,128)S(6)} %copy.10.count, s32[1,2]{1,0:T(1,128)} %bitcast.12, s32[1,2]{1,0:T(1,128)} %bitcast.13), custom_call_target="tpu_custom_call" | custom-call | tf_op jit(solution)/shard_map/pallas_call | solution.py:347
  47.6 0.8 %copy.9 = bf16[1,1,1280,256]{3,2,1,0:T(8,128)(2,1)} copy(bf16[1,1,1280,256]{3,2,1,0:T(8,128)(2,1)S(1)} %bitcast.7) | data formatting | bytes 1310720

commit v6 on v3

--- a/solution.py
+++ b/solution.py
@@ -48,7 +48,7 @@
 
 def sweep_kernel(
     sizes, source, blocks, ops_in, ops_out, count, ups_in, downs_in, result,
-    raw, trace, faces_in, edges_in, up_pick, down_pick, own_sum,
+    raw, trace, landed, up_pick, down_pick, own_sum,
     ops, merged, dense, in_list, out_list, in_row, out_row, table, places, ups, downs,
     load_sem, small_sem, table_sem, send_sem, recv_sem,
 ):
@@ -100,18 +100,18 @@
 
     @pl.when(jnp.logical_not(has_below))
     def _():
-        edges_in[:, :, 0:EMAX] = jnp.zeros((ITERS, CHUNKS, EMAX, width, bs), edges_in.dtype)
+        landed[:, :, 2 * FX : 2 * FX + EMAX] = jnp.zeros((ITERS, CHUNKS, EMAX, width, bs), landed.dtype)
 
     @pl.when(jnp.logical_not(has_above))
     def _():
-        edges_in[:, :, EMAX:] = jnp.zeros((ITERS, CHUNKS, EMAX, width, bs), edges_in.dtype)
+        landed[:, :, 2 * FX + EMAX :] = jnp.zeros((ITERS, CHUNKS, EMAX, width, bs), landed.dtype)
 
     def remote(t, c, which):
         src, dst, place = (
-            (trace.at[t, c, pl.ds(nb - FX, FX)], faces_in.at[t, c, pl.ds(0, FX)], right),
-            (trace.at[t, c, pl.ds(0, FX)], faces_in.at[t, c, pl.ds(FX, FX)], left),
-            (up_pick.at[t, c], edges_in.at[t, c, pl.ds(0, EMAX)], above),
-            (down_pick.at[t, c], edges_in.at[t, c, pl.ds(EMAX, EMAX)], below),
+            (trace.at[t, c, pl.ds(nb - FX, FX)], landed.at[t, c, pl.ds(0, FX)], right),
+            (trace.at[t, c, pl.ds(0, FX)], landed.at[t, c, pl.ds(FX, FX)], left),
+            (up_pick.at[t, c], landed.at[t, c, pl.ds(2 * FX, EMAX)], above),
+            (down_pick.at[t, c], landed.at[t, c, pl.ds(2 * FX + EMAX, EMAX)], below),
         )[which]
         return pltpu.make_async_remote_copy(
             src_ref=src,
@@ -135,19 +135,38 @@
                 down_pick[t, c, k] = trace[t, c, downs[0, k]]
             remote(t, c, 3).start()
 
-    def side_by_side(ref, t, c, count):
-        return jnp.concatenate([ref[t, c, j] for j in range(count)], axis=1)
-
-    def dot(inputs, first, end, first_out, end_out):
+    def side_by_side(ref, t, c, first, count):
+        return jnp.concatenate([ref[t, c, first + j] for j in range(count)], axis=1)
+
+    def dot(inputs, first, count, first_out, end_out):
         return jnp.dot(
             inputs,
-            dense[first * bs : end * bs, first_out * bs : end_out * bs],
+            dense[pl.ds(pl.multiple_of(first * bs, bs), count * bs), first_out * bs : end_out * bs],
             preferred_element_type=jnp.float32,
         )
 
+    crosses = jnp.logical_or(gy == n_gy // 2 - 1, gy == n_gy // 2)
+    sooner = jnp.where(crosses, 0, 2 * FX)
+    later = 2 * FX - sooner
+
+    def wait_edges(t, c, now):
+        @pl.when(jnp.logical_and(now, has_below))
+        def _():
+            remote(t, c, 2).wait_recv()
+
+        @pl.when(jnp.logical_and(now, has_above))
+        def _():
+            remote(t, c, 3).wait_recv()
+
+    def wait_faces(t, c, now):
+        @pl.when(now)
+        def _():
+            remote(t, c, 0).wait_recv()
+            remote(t, c, 1).wait_recv()
+
     def own_term(t, c):
-        terms = side_by_side(trace, 0, c, nb).astype(jnp.float32)
-        own_sum[c] = terms + dot(side_by_side(trace, t, c, nb), 0, nb, 0, nb)
+        terms = side_by_side(trace, 0, c, 0, nb).astype(jnp.float32)
+        own_sum[c] = terms + dot(side_by_side(trace, t, c, 0, nb), 0, nb, 0, nb)
 
     for c in range(CHUNKS):
         loads[c].wait()
@@ -184,25 +203,18 @@
 
     for t in range(ITERS):
         for c in range(CHUNKS):
-            @pl.when(has_below)
-            def _():
-                remote(t, c, 2).wait_recv()
-
-            @pl.when(has_above)
-            def _():
-                remote(t, c, 3).wait_recv()
-
+            wait_edges(t, c, jnp.logical_not(crosses))
+            wait_faces(t, c, crosses)
             own_sum[c] += dot(
-                side_by_side(edges_in, t, c, 2 * EMAX), nb + 2 * FX, ni, 0, nb
+                side_by_side(landed, t, c, sooner, 2 * FX), nb + sooner, 2 * FX, 0, nb
             )
-            remote(t, c, 0).wait_recv()
-            remote(t, c, 1).wait_recv()
-
-            faces = side_by_side(faces_in, t, c, 2 * FX)
+            wait_faces(t, c, jnp.logical_not(crosses))
+            wait_edges(t, c, crosses)
+            inputs = side_by_side(landed, t, c, later, 2 * FX)
 
             def finish(first, end):
                 total = own_sum[c, :, first * bs : end * bs] + dot(
-                    faces, nb, nb + 2 * FX, first, end
+                    inputs, nb + later, 2 * FX, first, end
                 )
                 if t == ITERS - 1:
                     result[:, c * width : (c + 1) * width] = total.T.astype(result.dtype)
@@ -256,8 +268,7 @@
         scratch_shapes=[
             pltpu.VMEM((CHUNKS, nb, bs, width), bf16),
             pltpu.VMEM((ITERS, CHUNKS, nb, width, bs), bf16),
-            pltpu.VMEM((ITERS, CHUNKS, 2 * FX, width, bs), bf16),
-            pltpu.VMEM((ITERS, CHUNKS, 2 * EMAX, width, bs), bf16),
+            pltpu.VMEM((ITERS, CHUNKS, 2 * FX + 2 * EMAX, width, bs), bf16),
             pltpu.VMEM((ITERS, CHUNKS, EMAX, width, bs), bf16),
             pltpu.VMEM((ITERS, CHUNKS, EMAX, width, bs), bf16),
             pltpu.VMEM((CHUNKS, width, rows), jnp.float32),

time: 47.6 us -> 46.8 us (0.983)
  Pallas kernels: 45.9 us -> 45.2 us
    pallas_call x1, Pallas kernels: 45.9 us -> 45.2 us  [shards(): pl.pallas_call(functools.partial(sweep_kernel, sizes), out_shape=pltpu.VM...]
where the time goes in v6:
time: 46.8 us; the launch traced here: 46.7 us
  Pallas kernels  45.2 us (97%)
  local copies, waits for them, and re-layouts  0.84 us (2%)
  between operations  0.66 us (1%)
    pallas_call x1, Pallas kernels, shards(): pl.pallas_call(functools.partial(sweep_kernel, sizes), out_shape=pltpu.VM...  45.2 us

profile of v6, /device:TPU:25, one launch (start us, length us, event | category | flops | bytes accessed | tf_op | source)
XLA Modules:
  0.0 46.7 jit_solution(13656370390027073303)
XLA Ops:
  0.7 45.2 %shard_map.73 = bf16[1280,256]{1,0:T(8,128)(2,1)S(1)} custom-call(bf16[10,128,256]{2,1,0:T(8,128)(2,1)} %bitcast.9, bf16[80,128,128]{2,1,0:T(8,128)(2,1)} %bitcast.8, s32[1,80]{1,0:T(1,128)} %bitcast.10, s32[1,80]{1,0:T(1,128)} %bitcast.11, s32[1,1]{1,0:T(1,128)S(6)} %copy.10.count, s32[1,2]{1,0:T(1,128)} %bitcast.12, s32[1,2]{1,0:T(1,128)} %bitcast.13), custom_call_target="tpu_custom_call" | custom-call | tf_op jit(solution)/shard_map/pallas_call | solution.py:263
  45.8 0.8 %copy.9 = bf16[1,1,1280,256]{3,2,1,0:T(8,128)(2,1)} copy(bf16[1,1,1280,256]{3,2,1,0:T(8,128)(2,1)S(1)} %bitcast.7) | data formatting | bytes 1310720
